TPU v7x, 32 devices: a whole 2x2x4 slice. The times are simulated.
32 devices in a mesh: seq: 16 (over z, x, core), dp: 2 (over y).
Axes of the slice: x: 2, y: 2, z: 4, core: 2. Of those that a mesh axis runs over, the one named last changes fastest.
Arguments:
- inputs: bfloat16 [2, 2048, 2048], P('dp', 'seq'), may hold values from -6 to 6
- filters: bfloat16 [2048, 2048], P('seq', 'dp'), may hold values from -6 to 6
- grad_out: bfloat16 [2, 2048, 2048], P('dp', 'seq'), may hold values from -0.125 to 0.125
Outputs:
- grad_inputs: bfloat16 [2, 2048, 2048], P('dp', 'seq')
- grad_filters: bfloat16 [2048, 2048], P('seq', 'dp')
All inputs are finite; a program needn't handle non-finite values.
Results may differ from a plain program's by a relative error of at most 0.001.
Values may be sent and summed in bfloat16 or wider, within the bound.
A program may use at most 128 MiB of HBM per device.

v0:
```python
import functools
import math

import jax
import jax.numpy as jnp
import ml_dtypes
import numpy as np
from jax import lax
from jax.experimental import pallas as pl
from jax.experimental.pallas import tpu as pltpu
from jax.sharding import PartitionSpec as P

exact_mode = lax.Precision.HIGHEST


def phases(left_index, right_index, modulus):
    product = left_index[:, None] * right_index[None, :] % modulus
    angles = 2.0 * math.pi / modulus * product.astype(jnp.float32)
    return (jnp.cos(angles), jnp.sin(angles))


def across(block_in, length_all):
    seq_parts = block_in.shape[0]
    slot_rows = block_in.shape[1]
    values = block_in.astype(jnp.float32)
    cosine, sine_table = phases(
        jnp.arange(2 * seq_parts, dtype=jnp.int32),
        jnp.arange(seq_parts, dtype=jnp.int32),
        2 * seq_parts,
    )
    real_part = jnp.einsum("kp,pjw->kjw", cosine, values, precision=exact_mode)
    imag_part = -jnp.einsum("kp,pjw->kjw", sine_table, values, precision=exact_mode)
    twist_cos, twist_sin = phases(
        jnp.arange(2 * seq_parts, dtype=jnp.int32),
        jnp.arange(slot_rows, dtype=jnp.int32),
        length_all,
    )
    twist_cos = twist_cos[:, :, None]
    twist_sin = twist_sin[:, :, None]
    return jnp.stack(
        [
            real_part * twist_cos + imag_part * twist_sin,
            imag_part * twist_cos - real_part * twist_sin,
        ]
    )


def along(spectra):
    row_count = spectra.shape[2]
    index_rows = jnp.arange(row_count, dtype=jnp.int32)
    cosine, sine_table = phases(index_rows, index_rows, row_count)
    cos_real = jnp.einsum("kn,rnw->rkw", cosine, spectra[0], precision=exact_mode)
    cos_imag = jnp.einsum("kn,rnw->rkw", cosine, spectra[1], precision=exact_mode)
    sin_real = jnp.einsum("kn,rnw->rkw", sine_table, spectra[0], precision=exact_mode)
    sin_imag = jnp.einsum("kn,rnw->rkw", sine_table, spectra[1], precision=exact_mode)
    return jnp.stack([cos_real + sin_imag, cos_imag - sin_real])


def back_along(spectra, length_all):
    row_count = spectra.shape[2]
    coarse = spectra.shape[1]
    index_rows = jnp.arange(row_count, dtype=jnp.int32)
    cosine, sine_table = phases(index_rows, index_rows, row_count)
    cos_real = jnp.einsum("nk,rkw->rnw", cosine, spectra[0], precision=exact_mode)
    cos_imag = jnp.einsum("nk,rkw->rnw", cosine, spectra[1], precision=exact_mode)
    sin_real = jnp.einsum("nk,rkw->rnw", sine_table, spectra[0], precision=exact_mode)
    sin_imag = jnp.einsum("nk,rkw->rnw", sine_table, spectra[1], precision=exact_mode)
    inner_real = cos_real - sin_imag
    inner_imag = cos_imag + sin_real
    twist_cos, twist_sin = phases(jnp.arange(coarse, dtype=jnp.int32), index_rows, length_all)
    twist_cos = twist_cos[:, :, None]
    twist_sin = twist_sin[:, :, None]
    return jnp.stack(
        [
            inner_real * twist_cos - inner_imag * twist_sin,
            inner_imag * twist_cos + inner_real * twist_sin,
        ]
    )


def collapse(spectra, length_all):
    coarse = spectra.shape[1]
    seq_parts = coarse // 2
    cosine, sine_table = phases(
        jnp.arange(seq_parts, dtype=jnp.int32), jnp.arange(coarse, dtype=jnp.int32), coarse
    )
    values = jnp.einsum("nk,kjw->njw", cosine, spectra[0], precision=exact_mode)
    values = values - jnp.einsum("nk,kjw->njw", sine_table, spectra[1], precision=exact_mode)
    return values * (1.0 / length_all)


def paired(left_spec, right_spec):
    real_part = left_spec[0] * right_spec[0] + left_spec[1] * right_spec[1]
    imag_part = left_spec[0] * right_spec[1] - left_spec[1] * right_spec[0]
    return jnp.stack([real_part, imag_part])


def spread(matrix, dp_groups, seq_parts):
    row_count = matrix.shape[0]
    narrow = matrix.shape[1] // (dp_groups * seq_parts)
    return jnp.transpose(matrix.reshape(row_count, dp_groups, seq_parts, narrow), (0, 2, 1, 3))


def per_device(inputs, filters, grad_out):
    row_count = inputs.shape[1]
    channels = inputs.shape[2]
    seq_parts = lax.axis_size("seq")
    dp_groups = lax.axis_size("dp")
    length_all = 2 * seq_parts * row_count
    signal = inputs[0]
    cotangent = grad_out[0]
    whole_filter = lax.all_gather(filters, "dp", axis=1, tiled=True)
    narrow = channels // (dp_groups * seq_parts)
    stacked = jnp.stack(
        [
            spread(signal, dp_groups, seq_parts),
            spread(cotangent, dp_groups, seq_parts),
            spread(whole_filter, dp_groups, seq_parts),
        ],
        axis=2,
    )
    moved_rows = lax.all_to_all(stacked, "seq", split_axis=1, concat_axis=0, tiled=True)
    local_grid = moved_rows.reshape(seq_parts, row_count, 3 * dp_groups * narrow)
    spectra = along(across(local_grid, length_all))
    spectra = spectra.reshape(2, 2 * seq_parts, row_count, 3, dp_groups, narrow)
    input_spec = paired(spectra[:, :, :, 2], spectra[:, :, :, 1])
    filter_spec = paired(spectra[:, :, :, 0], spectra[:, :, :, 1])
    joined = jnp.concatenate([input_spec, filter_spec], axis=3)
    slot_count = joined.shape[3]
    flattened = joined.reshape(2, joined.shape[1], row_count, slot_count * narrow)
    result = collapse(back_along(flattened, length_all), length_all).reshape(
        seq_parts * row_count, slot_count, narrow
    )
    grad_in = result[:, :dp_groups]
    grad_filter = lax.psum_scatter(result[:, dp_groups:], "dp", scatter_dimension=1, tiled=True)
    outgoing = jnp.concatenate([grad_in, grad_filter], axis=1).astype(jnp.bfloat16)
    outgoing = outgoing.reshape(seq_parts * row_count, 1, dp_groups + 1, narrow)
    returned = lax.all_to_all(outgoing, "seq", split_axis=0, concat_axis=1, tiled=True)
    grad_inputs = jnp.transpose(returned[:, :, :dp_groups], (0, 2, 1, 3)).reshape(
        1, row_count, channels
    )
    grad_filters = returned[:, :, dp_groups].reshape(row_count, channels // dp_groups)
    return (grad_inputs, grad_filters)


lanes = 128
tile_rows = 16
f32 = jnp.float32
bf16 = jnp.bfloat16


def tables(parts, rows):
    total = 2 * parts * rows
    coarse = np.arange(parts + 1)[:, None, None]
    fine = np.arange(rows)[None, :, None]
    index = np.arange(rows)[None, None, :]
    angle = 2.0 * np.pi / total * (index * (coarse + 2 * parts * fine) % total)
    cosine, sine = np.cos(angle), np.sin(angle)
    forward = np.concatenate(
        [
            np.concatenate([cosine, sine], axis=2),
            np.concatenate([-sine, cosine], axis=2),
        ],
        axis=1,
    )
    weight = np.where((np.arange(parts + 1) % parts) == 0, 1.0, 2.0) / total
    backward = np.transpose(forward, (0, 2, 1)) * weight[:, None, None]

    def two_terms(matrix):
        high = matrix.astype(ml_dtypes.bfloat16)
        low = (matrix - high.astype(np.float64)).astype(ml_dtypes.bfloat16)
        return np.stack([high, low], axis=1)

    return two_terms(forward), two_terms(backward)


def spread_dft(values):
    count = len(values)
    if count == 1:
        return [(values[0], None), (values[0], None)]
    even, odd = spread_dft(values[0::2]), spread_dft(values[1::2])
    half = count // 2
    out = [None] * (count + 1)
    out[0] = (even[0][0] + odd[0][0], None)
    out[count] = (even[0][0] - odd[0][0], None)
    for k in range(1, half):
        c, s = math.cos(math.pi * k / count), math.sin(math.pi * k / count)
        real = odd[k][0] * c + odd[k][1] * s
        imag = odd[k][1] * c - odd[k][0] * s
        out[k] = (even[k][0] + real, even[k][1] + imag)
        out[count - k] = (even[k][0] - real, imag - even[k][1])
    out[half] = (even[half][0], -odd[half][0])
    return out


def gather_dft(spectrum):
    count = len(spectrum) - 1
    if count == 1:
        return [spectrum[0][0] + spectrum[1][0]]
    half = count // 2
    even, odd = [None] * (half + 1), [None] * (half + 1)
    even[0] = (spectrum[0][0] + spectrum[count][0], None)
    odd[0] = (spectrum[0][0] - spectrum[count][0], None)
    for k in range(1, half):
        c, s = math.cos(math.pi * k / count), math.sin(math.pi * k / count)
        ar, ai = spectrum[k]
        br, bi = spectrum[count - k]
        even[k] = (ar + br, ai - bi)
        dr, di = ar - br, ai + bi
        odd[k] = (dr * c - di * s, di * c + dr * s)
    even[half] = (spectrum[half][0], None)
    odd[half] = (-spectrum[half][1], None)
    out = [None] * count
    out[0::2] = gather_dft(even)
    out[1::2] = gather_dft(odd)
    return out


def two_terms_of(value):
    high = value.astype(bf16)
    return high, (value - high.astype(f32)).astype(bf16)


def exact_dot(table, k, high, low):
    dot = functools.partial(jnp.dot, preferred_element_type=f32)
    return dot(table[k, 0], high) + dot(table[k, 0], low) + dot(table[k, 1], high)


def kernel(
    parts,
    x_ref,
    g_ref,
    f_ref,
    fwd_hbm,
    inv_hbm,
    gi_ref,
    gf_ref,
    fwd,
    inv,
    xs,
    gs,
    fs,
    xr,
    gr,
    fr,
    gis,
    gfs,
    gir,
    gfr,
    fg_high,
    fg_low,
    x_high,
    x_low,
    g_spec,
    inner,
    table_sem,
    xs_sem,
    xr_sem,
    gs_sem,
    gr_sem,
    fs_sem,
    fr_sem,
    gis_sem,
    gir_sem,
    gfs_sem,
    gfr_sem,
):
    me_s, me_d = lax.axis_index("seq"), lax.axis_index("dp")
    everyone = 2 * parts
    me = me_s * 2 + me_d
    own = me_d * parts + me_s
    rows = x_ref.shape[0]
    half = rows // 2
    low_half = lax.broadcasted_iota(jnp.int32, (half, lanes), 1) < lanes // 2
    low_tile = lax.broadcasted_iota(jnp.int32, (tile_rows, lanes), 1) < lanes // 2

    def swap(mask, first, second):
        return (
            jnp.where(mask, first, pltpu.roll(second, lanes // 2, 1)),
            jnp.where(mask, pltpu.roll(first, lanes // 2, 1), second),
        )

    def loop(start, stop, body):
        def step(i, carry):
            body(i)
            return carry

        lax.fori_loop(start, stop, step, 0)

    def partner(o):
        other = lax.rem(me + o, everyone)
        return lax.div(other, 2), lax.rem(other, 2)

    def peer(o):
        return lax.rem(me_s + o, parts)

    barrier = pltpu.get_barrier_semaphore()

    def greet(o):
        s, d = partner(o)
        pl.semaphore_signal(
            barrier, inc=1, device_id=(s, d), device_id_type=pl.DeviceIdType.MESH
        )

    loop(1, everyone, greet)
    fwd_copy = pltpu.make_async_copy(fwd_hbm, fwd, table_sem.at[0])
    inv_copy = pltpu.make_async_copy(inv_hbm, inv, table_sem.at[1])
    fwd_copy.start()
    inv_copy.start()

    def pack(source, target):
        def step(m):
            column = pl.ds(pl.multiple_of(m * lanes, lanes), lanes)
            first, second = swap(
                low_half,
                source[0:half, column].astype(f32),
                source[half:rows, column].astype(f32),
            )
            target[2 * m] = first.astype(bf16)
            target[2 * m + 1] = second.astype(bf16)

        loop(0, source.shape[1] // lanes, step)

    def unpack(source, target):
        def step(m):
            column = pl.ds(pl.multiple_of(m * lanes, lanes), lanes)
            first, second = swap(
                low_half, source[2 * m].astype(f32), source[2 * m + 1].astype(f32)
            )
            target[0:half, column] = first.astype(bf16)
            target[half:rows, column] = second.astype(bf16)

        loop(0, target.shape[1] // lanes, step)

    def to_all(source, target, send, receive):
        def copy(o):
            s, d = partner(o)
            return pltpu.make_async_remote_copy(
                src_ref=source.at[d * parts + s],
                dst_ref=target.at[own],
                send_sem=send.at[d * parts + s],
                recv_sem=receive.at[own],
                device_id=(s, d),
                device_id_type=pl.DeviceIdType.MESH,
            )

        def arrived(o):
            s, d = partner(o)
            pltpu.make_async_remote_copy(
                src_ref=source.at[own],
                dst_ref=target.at[d * parts + s],
                send_sem=send.at[own],
                recv_sem=receive.at[d * parts + s],
                device_id=(s, d),
                device_id_type=pl.DeviceIdType.MESH,
            ).wait_recv()

        def start():
            loop(1, everyone, lambda o: copy(o).start())
            target[own] = source[own]

        def wait():
            loop(1, everyone, arrived)

        def sent():
            loop(1, everyone, lambda o: copy(o).wait_send())

        return start, wait, sent

    def to_row(source, target, send, receive):
        def copy(o):
            return pltpu.make_async_remote_copy(
                src_ref=source.at[peer(o)],
                dst_ref=target.at[me_s],
                send_sem=send.at[peer(o)],
                recv_sem=receive.at[me_s],
                device_id=(peer(o), me_d),
                device_id_type=pl.DeviceIdType.MESH,
            )

        def arrived(o):
            pltpu.make_async_remote_copy(
                src_ref=source.at[me_s],
                dst_ref=target.at[peer(o)],
                send_sem=send.at[me_s],
                recv_sem=receive.at[peer(o)],
                device_id=(peer(o), me_d),
                device_id_type=pl.DeviceIdType.MESH,
            ).wait_recv()

        def start():
            loop(1, parts, lambda o: copy(o).start())
            target[me_s] = source[me_s]

        def wait():
            loop(1, parts, arrived)

        def sent():
            loop(1, parts, lambda o: copy(o).wait_send())

        return start, wait, sent

    f_start, f_wait, f_sent = to_row(fs, fr, fs_sem, fr_sem)
    g_start, g_wait, g_sent = to_all(gs, gr, gs_sem, gr_sem)
    x_start, x_wait, x_sent = to_all(xs, xr, xs_sem, xr_sem)
    gi_start, gi_wait, gi_sent = to_all(gis, gir, gis_sem, gir_sem)
    gf_start, gf_wait, gf_sent = to_row(gfs, gfr, gfs_sem, gfr_sem)

    pack(f_ref, fs)
    pack(g_ref, gs)
    pl.semaphore_wait(barrier, everyone - 1)
    f_start()
    g_start()
    pack(x_ref, xs)
    x_start()

    zeros = jnp.zeros((rows, lanes), bf16)

    def spread_to(load, high, low, lane_at):
        columns = slice(lane_at, lane_at + lanes)
        for k in (0, parts):
            high[k, rows:, columns] = zeros
            low[k, rows:, columns] = zeros

        def step(t):
            at = pl.multiple_of(t * tile_rows, tile_rows)
            for side in range(2):
                values = [load(p, pl.ds(at, tile_rows))[side] for p in range(parts)]
                for k, (real, imag) in enumerate(spread_dft(values)):
                    where = pl.ds(side * half + at, tile_rows)
                    high[k, where, columns], low[k, where, columns] = two_terms_of(real)
                    if imag is not None:
                        where = pl.ds(rows + side * half + at, tile_rows)
                        high[k, where, columns], low[k, where, columns] = two_terms_of(imag)

        loop(0, half // tile_rows, step)

    def load_pair(source):
        def load(p, where):
            return swap(
                low_tile, source[p, where].astype(f32), source[parts + p, where].astype(f32)
            )

        return load

    def load_twice(p, where):
        value = fr[p, where].astype(f32)
        return swap(low_tile, value, value)

    def product(left, right):
        lr, li, rr, ri = left[:rows], left[rows:], right[:rows], right[rows:]
        return two_terms_of(
            jnp.concatenate([lr * rr + li * ri, lr * ri - li * rr], axis=0)
        )

    def gather_from(store):
        def step(t):
            at = pl.multiple_of(t * tile_rows, tile_rows)
            found = []
            for side in range(2):
                spectrum = []
                for k in range(parts + 1):
                    real = inner[k, pl.ds(side * half + at, tile_rows)]
                    imag = None
                    if k % parts:
                        imag = inner[k, pl.ds(rows + side * half + at, tile_rows)]
                    spectrum.append((real, imag))
                found.append(gather_dft(spectrum))
            for q in range(parts):
                store(q, pl.ds(at, tile_rows), found[0][q], found[1][q])

        loop(0, half // tile_rows, step)

    f_wait()
    spread_to(load_twice, fg_high, fg_low, 0)
    g_wait()
    spread_to(load_pair(gr), fg_high, fg_low, lanes)
    fwd_copy.wait()
    inv_copy.wait()

    def input_step(k):
        both = exact_dot(fwd, k, fg_high[k], fg_low[k])
        right = both[:, lanes:]
        g_spec[k] = right
        inner[k] = exact_dot(inv, k, *product(both[:, :lanes], right))

    loop(0, parts + 1, input_step)

    def store_input(q, where, top, bottom):
        first, second = swap(low_tile, top, bottom)
        gis[q, where] = first.astype(bf16)
        gis[parts + q, where] = second.astype(bf16)

    gather_from(store_input)
    gi_start()

    x_wait()
    spread_to(load_pair(xr), x_high, x_low, 0)

    def filter_step(k):
        left = exact_dot(fwd, k, x_high[k], x_low[k])
        inner[k] = exact_dot(inv, k, *product(left, g_spec[k]))

    loop(0, parts + 1, filter_step)

    def store_filter(q, where, top, bottom):
        first, second = swap(low_tile, top, bottom)
        gfs[q, where] = (first + second).astype(bf16)

    gather_from(store_filter)
    gf_start()

    gi_wait()
    unpack(gir, gi_ref)
    gf_wait()
    unpack(gfr, gf_ref)
    for sent in (f_sent, g_sent, x_sent, gi_sent, gf_sent):
        sent()


def whole_kernel(inputs, filters, grad_out):
    rows, channels = inputs.shape[1], inputs.shape[2]
    parts = lax.axis_size("seq")
    forward, backward = tables(parts, rows)
    half = rows // 2
    every = lambda: pltpu.VMEM((2 * parts, half, lanes), bf16)
    row = lambda: pltpu.VMEM((parts, half, lanes), bf16)
    spec = lambda width, dtype: pltpu.VMEM((parts + 1, 2 * rows, width), dtype)
    sems = lambda count: pltpu.SemaphoreType.DMA((count,))
    vmem = pl.BlockSpec(memory_space=pltpu.VMEM)
    hbm = pl.BlockSpec(memory_space=pl.ANY)
    grad_in, grad_filter = pl.pallas_call(
        functools.partial(kernel, parts),
        out_shape=(
            jax.ShapeDtypeStruct((rows, channels), bf16),
            jax.ShapeDtypeStruct(filters.shape, bf16),
        ),
        in_specs=[vmem, vmem, vmem, hbm, hbm],
        out_specs=(vmem, vmem),
        scratch_shapes=[
            pltpu.VMEM(forward.shape, bf16),
            pltpu.VMEM(backward.shape, bf16),
            every(),
            every(),
            row(),
            every(),
            every(),
            row(),
            every(),
            row(),
            every(),
            row(),
            spec(2 * lanes, bf16),
            spec(2 * lanes, bf16),
            spec(lanes, bf16),
            spec(lanes, bf16),
            spec(lanes, f32),
            spec(lanes, f32),
            sems(2),
            sems(2 * parts),
            sems(2 * parts),
            sems(2 * parts),
            sems(2 * parts),
            sems(parts),
            sems(parts),
            sems(2 * parts),
            sems(2 * parts),
            sems(parts),
            sems(parts),
        ],
        compiler_params=pltpu.CompilerParams(
            collective_id=0, has_side_effects=True, vmem_limit_bytes=50 * 2**20
        ),
    )(inputs[0], grad_out[0], filters, jnp.asarray(forward), jnp.asarray(backward))
    return grad_in[None], grad_filter


def choose(inputs, filters, grad_out):
    rows, channels = inputs.shape[1], inputs.shape[2]
    parts, groups = lax.axis_size("seq"), lax.axis_size("dp")
    fits = (
        groups == 2
        and channels == lanes // 2 * groups * parts
        and rows % (2 * tile_rows) == 0
        and parts % 2 == 0
        and parts <= 16
        and rows <= 128
    )
    return (whole_kernel if fits else per_device)(inputs, filters, grad_out)


def solution(mesh):
    return jax.shard_map(
        choose,
        mesh=mesh,
        in_specs=(P("dp", "seq", None), P("seq", "dp"), P("dp", "seq", None)),
        out_specs=(P("dp", "seq", None), P("seq", "dp")),
        check_vma=False,
    )
```

profile of v0, /device:TPU:25, one launch (start us, length us, event | category | flops | bytes accessed | tf_op | source)
XLA Modules:
  0.0 71.1 jit_solution(7619060756197060957)
XLA Ops:
  0.6 0.0 copy-start
  0.6 1.0 %copy-done = bf16[1,128,2048]{2,1,0:T(8,128)(2,1)S(1)} copy-done((bf16[1,128,2048]{2,1,0:T(8,128)(2,1)S(1)}, bf16[1,128,2048]{2,1,0:T(8,128)(2,1)}, u32[]{:S(2)}) %copy-start) | copy-done | bytes 524312
  1.7 0.0 copy-start.1
  1.7 1.0 %copy-done.1 = bf16[1,128,2048]{2,1,0:T(8,128)(2,1)S(1)} copy-done((bf16[1,128,2048]{2,1,0:T(8,128)(2,1)S(1)}, bf16[1,128,2048]{2,1,0:T(8,128)(2,1)}, u32[]{:S(2)}) %copy-start.1) | copy-done | bytes 524312
  2.7 0.0 copy-start.2
  2.7 0.9 %copy-done.2 = bf16[128,1024]{1,0:T(8,128)(2,1)S(1)} copy-done((bf16[128,1024]{1,0:T(8,128)(2,1)S(1)}, bf16[128,1024]{1,0:T(8,128)(2,1)}, u32[]{:S(2)}) %copy-start.2) | copy-done | bytes 262168
  3.7 65.9 %shard_map.68 = (bf16[128,2048]{1,0:T(8,128)(2,1)S(1)}, bf16[128,1024]{1,0:T(8,128)(2,1)S(1)}) custom-call(bf16[128,2048]{1,0:T(8,128)(2,1)S(1)} %bitcast.3, bf16[128,2048]{1,0:T(8,128)(2,1)S(1)} %bitcast.4, bf16[128,1024]{1,0:T(8,128)(2,1)S(1)} %copy-done.2, bf16[17,2,256,256]{3,2,1,0:T(8,128)(2,1)} %constant.4.clone.fwd_hbm, ...), custom_call_target="tpu_custom_call" | custom-call | tf_op jit(solution)/shard_map/pallas_call | solution.py:532
  69.6 0.8 %copy.9 = bf16[1,128,2048]{2,1,0:T(8,128)(2,1)} copy(bf16[1,128,2048]{2,1,0:T(8,128)(2,1)S(1)} %bitcast.5) | data formatting | bytes 1048576
  70.4 0.7 copy.10
Async XLA Ops:
  0.6 1.0 %copy-start = (bf16[1,128,2048]{2,1,0:T(8,128)(2,1)S(1)}, bf16[1,128,2048]{2,1,0:T(8,128)(2,1)}, u32[]{:S(2)}) copy-start(bf16[1,128,2048]{2,1,0:T(8,128)(2,1)} %param.5) | copy-start | bytes 1572868
  1.7 1.0 %copy-start.1 = (bf16[1,128,2048]{2,1,0:T(8,128)(2,1)S(1)}, bf16[1,128,2048]{2,1,0:T(8,128)(2,1)}, u32[]{:S(2)}) copy-start(bf16[1,128,2048]{2,1,0:T(8,128)(2,1)} %param.7) | copy-start | bytes 1572868
  2.7 0.9 %copy-start.2 = (bf16[128,1024]{1,0:T(8,128)(2,1)S(1)}, bf16[128,1024]{1,0:T(8,128)(2,1)}, u32[]{:S(2)}) copy-start(bf16[128,1024]{1,0:T(8,128)(2,1)} %f_ref.1) | copy-start | bytes 786436
where the time goes:
time: 71.9 us; the launch traced here: 71.1 us
  Pallas kernels  65.9 us (92%)
  local copies, waits for them, and re-layouts  4.52 us (6%)
    pallas_call x1, Pallas kernels, whole_kernel(): pl.pallas_call(functools.partial(kernel, parts), out_shape=(jax.ShapeDtyp...  65.9 us
    unnamed x8, local copies, waits for them, and re-layouts  4.52 us

commit v1 on v0

--- a/solution.py
+++ b/solution.py
@@ -145,6 +145,7 @@
 
 lanes = 128
 tile_rows = 16
+group = 4
 f32 = jnp.float32
 bf16 = jnp.bfloat16
 
@@ -169,7 +170,7 @@
     def two_terms(matrix):
         high = matrix.astype(ml_dtypes.bfloat16)
         low = (matrix - high.astype(np.float64)).astype(ml_dtypes.bfloat16)
-        return np.stack([high, low], axis=1)
+        return np.concatenate([high, low], axis=1)
 
     return two_terms(forward), two_terms(backward)
 
@@ -223,18 +224,28 @@
 
 def exact_dot(table, k, high, low):
     dot = functools.partial(jnp.dot, preferred_element_type=f32)
-    return dot(table[k, 0], high) + dot(table[k, 0], low) + dot(table[k, 1], high)
+    size = table.shape[2]
+    if high.shape[1] == lanes:
+        four = dot(table[k], jnp.concatenate([high, low], axis=1))
+        return four[:size, :lanes] + (four[:size, lanes:] + four[size:, :lanes])
+    two = dot(table[k], high)
+    return two[:size] + (two[size:] + dot(table[k, :size], low))
 
 
 def kernel(
     parts,
+    x_hbm,
+    g_hbm,
+    f_hbm,
+    fwd_hbm,
+    inv_hbm,
+    gi_hbm,
+    gf_hbm,
+    gi_ref,
+    gf_ref,
     x_ref,
     g_ref,
     f_ref,
-    fwd_hbm,
-    inv_hbm,
-    gi_ref,
-    gf_ref,
     fwd,
     inv,
     xs,
@@ -291,9 +302,6 @@
         other = lax.rem(me + o, everyone)
         return lax.div(other, 2), lax.rem(other, 2)
 
-    def peer(o):
-        return lax.rem(me_s + o, parts)
-
     barrier = pltpu.get_barrier_semaphore()
 
     def greet(o):
@@ -302,24 +310,27 @@
             barrier, inc=1, device_id=(s, d), device_id_type=pl.DeviceIdType.MESH
         )
 
-    loop(1, everyone, greet)
+    f_copy = pltpu.make_async_copy(f_hbm, f_ref, table_sem.at[2])
+    g_copy = pltpu.make_async_copy(g_hbm, g_ref, table_sem.at[3])
+    x_copy = pltpu.make_async_copy(x_hbm, x_ref, table_sem.at[4])
     fwd_copy = pltpu.make_async_copy(fwd_hbm, fwd, table_sem.at[0])
     inv_copy = pltpu.make_async_copy(inv_hbm, inv, table_sem.at[1])
+    f_copy.start()
+    g_copy.start()
+    x_copy.start()
+    loop(1, everyone, greet)
     fwd_copy.start()
     inv_copy.start()
 
-    def pack(source, target):
-        def step(m):
-            column = pl.ds(pl.multiple_of(m * lanes, lanes), lanes)
-            first, second = swap(
-                low_half,
-                source[0:half, column].astype(f32),
-                source[half:rows, column].astype(f32),
-            )
-            target[2 * m] = first.astype(bf16)
-            target[2 * m + 1] = second.astype(bf16)
-
-        loop(0, source.shape[1] // lanes, step)
+    def pack(source, target, m):
+        column = pl.ds(pl.multiple_of(m * lanes, lanes), lanes)
+        first, second = swap(
+            low_half,
+            source[0:half, column].astype(f32),
+            source[half:rows, column].astype(f32),
+        )
+        target[2 * m] = first.astype(bf16)
+        target[2 * m + 1] = second.astype(bf16)
 
     def unpack(source, target):
         def step(m):
@@ -332,73 +343,46 @@
 
         loop(0, target.shape[1] // lanes, step)
 
-    def to_all(source, target, send, receive):
-        def copy(o):
-            s, d = partner(o)
-            return pltpu.make_async_remote_copy(
-                src_ref=source.at[d * parts + s],
-                dst_ref=target.at[own],
-                send_sem=send.at[d * parts + s],
-                recv_sem=receive.at[own],
-                device_id=(s, d),
+    def exchange(source, target, send, receive, mine, device_of):
+        count = source.shape[0]
+
+        def start(i):
+            pltpu.make_async_remote_copy(
+                src_ref=source.at[i],
+                dst_ref=target.at[mine],
+                send_sem=send.at[0],
+                recv_sem=receive.at[0],
+                device_id=device_of(i),
                 device_id_type=pl.DeviceIdType.MESH,
-            )
-
-        def arrived(o):
-            s, d = partner(o)
-            pltpu.make_async_remote_copy(
-                src_ref=source.at[own],
-                dst_ref=target.at[d * parts + s],
-                send_sem=send.at[own],
-                recv_sem=receive.at[d * parts + s],
-                device_id=(s, d),
-                device_id_type=pl.DeviceIdType.MESH,
-            ).wait_recv()
-
-        def start():
-            loop(1, everyone, lambda o: copy(o).start())
-            target[own] = source[own]
-
-        def wait():
-            loop(1, everyone, arrived)
-
-        def sent():
-            loop(1, everyone, lambda o: copy(o).wait_send())
-
-        return start, wait, sent
-
-    def to_row(source, target, send, receive):
-        def copy(o):
-            return pltpu.make_async_remote_copy(
-                src_ref=source.at[peer(o)],
-                dst_ref=target.at[me_s],
-                send_sem=send.at[peer(o)],
-                recv_sem=receive.at[me_s],
-                device_id=(peer(o), me_d),
-                device_id_type=pl.DeviceIdType.MESH,
-            )
-
-        def arrived(o):
-            pltpu.make_async_remote_copy(
-                src_ref=source.at[me_s],
-                dst_ref=target.at[peer(o)],
-                send_sem=send.at[me_s],
-                recv_sem=receive.at[peer(o)],
-                device_id=(peer(o), me_d),
-                device_id_type=pl.DeviceIdType.MESH,
-            ).wait_recv()
-
-        def start():
-            loop(1, parts, lambda o: copy(o).start())
-            target[me_s] = source[me_s]
-
-        def wait():
-            loop(1, parts, arrived)
-
-        def sent():
-            loop(1, parts, lambda o: copy(o).wait_send())
-
-        return start, wait, sent
+            ).start()
+
+        def pair(step, before):
+            m = lax.rem(lax.div(mine, 2) + step, count // 2)
+            if before is not None:
+                before(m)
+            for i in (2 * m, 2 * m + 1):
+                pl.when(i != mine)(functools.partial(start, i))
+
+        def start_all(before=None):
+            loop(0, count // 2, lambda step: pair(step, before))
+            target[mine] = source[mine]
+
+        others = pl.ds(0, count - 1)
+        everything = pltpu.make_async_remote_copy(
+            src_ref=source.at[others],
+            dst_ref=target.at[others],
+            send_sem=send.at[0],
+            recv_sem=receive.at[0],
+            device_id=device_of(lax.rem(mine + 1, count)),
+            device_id_type=pl.DeviceIdType.MESH,
+        )
+        return start_all, everything.wait_recv, everything.wait_send
+
+    def to_all(*refs):
+        return exchange(*refs, own, lambda i: (lax.rem(i, parts), lax.div(i, parts)))
+
+    def to_row(*refs):
+        return exchange(*refs, me_s, lambda i: (i, me_d))
 
     f_start, f_wait, f_sent = to_row(fs, fr, fs_sem, fr_sem)
     g_start, g_wait, g_sent = to_all(gs, gr, gs_sem, gr_sem)
@@ -406,13 +390,13 @@
     gi_start, gi_wait, gi_sent = to_all(gis, gir, gis_sem, gir_sem)
     gf_start, gf_wait, gf_sent = to_row(gfs, gfr, gfs_sem, gfr_sem)
 
-    pack(f_ref, fs)
-    pack(g_ref, gs)
+    f_copy.wait()
+    g_copy.wait()
     pl.semaphore_wait(barrier, everyone - 1)
-    f_start()
-    g_start()
-    pack(x_ref, xs)
-    x_start()
+    f_start(lambda m: pack(f_ref, fs, m))
+    g_start(lambda m: pack(g_ref, gs, m))
+    x_copy.wait()
+    x_start(lambda m: pack(x_ref, xs, m))
 
     zeros = jnp.zeros((rows, lanes), bf16)
 
@@ -452,6 +436,10 @@
         return two_terms_of(
             jnp.concatenate([lr * rr + li * ri, lr * ri - li * rr], axis=0)
         )
+
+    def in_groups(step):
+        loop(0, parts // group, lambda g: step([g * group + j for j in range(group)]))
+        step([parts])
 
     def gather_from(store):
         def step(t):
@@ -478,13 +466,15 @@
     fwd_copy.wait()
     inv_copy.wait()
 
-    def input_step(k):
-        both = exact_dot(fwd, k, fg_high[k], fg_low[k])
-        right = both[:, lanes:]
-        g_spec[k] = right
-        inner[k] = exact_dot(inv, k, *product(both[:, :lanes], right))
-
-    loop(0, parts + 1, input_step)
+    def input_step(ks):
+        both = [exact_dot(fwd, k, fg_high[k], fg_low[k]) for k in ks]
+        for k, spectrum in zip(ks, both):
+            g_spec[k] = spectrum[:, lanes:]
+        terms = [product(spectrum[:, :lanes], spectrum[:, lanes:]) for spectrum in both]
+        for k, term in zip(ks, terms):
+            inner[k] = exact_dot(inv, k, *term)
+
+    in_groups(input_step)
 
     def store_input(q, where, top, bottom):
         first, second = swap(low_tile, top, bottom)
@@ -497,11 +487,13 @@
     x_wait()
     spread_to(load_pair(xr), x_high, x_low, 0)
 
-    def filter_step(k):
-        left = exact_dot(fwd, k, x_high[k], x_low[k])
-        inner[k] = exact_dot(inv, k, *product(left, g_spec[k]))
-
-    loop(0, parts + 1, filter_step)
+    def filter_step(ks):
+        left = [exact_dot(fwd, k, x_high[k], x_low[k]) for k in ks]
+        terms = [product(spectrum, g_spec[k]) for k, spectrum in zip(ks, left)]
+        for k, term in zip(ks, terms):
+            inner[k] = exact_dot(inv, k, *term)
+
+    in_groups(filter_step)
 
     def store_filter(q, where, top, bottom):
         first, second = swap(low_tile, top, bottom)
@@ -510,12 +502,21 @@
     gather_from(store_filter)
     gf_start()
 
+    f_sent()
+    g_sent()
+    x_sent()
     gi_wait()
     unpack(gir, gi_ref)
+    gi_copy = pltpu.make_async_copy(gi_ref, gi_hbm, table_sem.at[5])
+    gi_copy.start()
+    gi_sent()
     gf_wait()
     unpack(gfr, gf_ref)
-    for sent in (f_sent, g_sent, x_sent, gi_sent, gf_sent):
-        sent()
+    gf_copy = pltpu.make_async_copy(gf_ref, gf_hbm, table_sem.at[6])
+    gf_copy.start()
+    gf_sent()
+    gi_copy.wait()
+    gf_copy.wait()
 
 
 def whole_kernel(inputs, filters, grad_out):
@@ -527,17 +528,21 @@
     row = lambda: pltpu.VMEM((parts, half, lanes), bf16)
     spec = lambda width, dtype: pltpu.VMEM((parts + 1, 2 * rows, width), dtype)
     sems = lambda count: pltpu.SemaphoreType.DMA((count,))
-    vmem = pl.BlockSpec(memory_space=pltpu.VMEM)
-    hbm = pl.BlockSpec(memory_space=pl.ANY)
+    hbm = pl.BlockSpec(memory_space=pltpu.HBM)
     grad_in, grad_filter = pl.pallas_call(
         functools.partial(kernel, parts),
         out_shape=(
             jax.ShapeDtypeStruct((rows, channels), bf16),
             jax.ShapeDtypeStruct(filters.shape, bf16),
         ),
-        in_specs=[vmem, vmem, vmem, hbm, hbm],
-        out_specs=(vmem, vmem),
+        in_specs=[hbm] * 5,
+        out_specs=(hbm, hbm),
         scratch_shapes=[
+            pltpu.VMEM((rows, channels), bf16),
+            pltpu.VMEM(filters.shape, bf16),
+            pltpu.VMEM((rows, channels), bf16),
+            pltpu.VMEM((rows, channels), bf16),
+            pltpu.VMEM(filters.shape, bf16),
             pltpu.VMEM(forward.shape, bf16),
             pltpu.VMEM(backward.shape, bf16),
             every(),
@@ -556,20 +561,11 @@
             spec(lanes, bf16),
             spec(lanes, f32),
             spec(lanes, f32),
-            sems(2),
-            sems(2 * parts),
-            sems(2 * parts),
-            sems(2 * parts),
-            sems(2 * parts),
-            sems(parts),
-            sems(parts),
-            sems(2 * parts),
-            sems(2 * parts),
-            sems(parts),
-            sems(parts),
+            sems(7),
+            *[sems(1) for _ in range(10)],
         ],
         compiler_params=pltpu.CompilerParams(
-            collective_id=0, has_side_effects=True, vmem_limit_bytes=50 * 2**20
+            collective_id=0, has_side_effects=True, vmem_limit_bytes=60 * 2**20
         ),
     )(inputs[0], grad_out[0], filters, jnp.asarray(forward), jnp.asarray(backward))
     return grad_in[None], grad_filter
@@ -582,7 +578,7 @@
         groups == 2
         and channels == lanes // 2 * groups * parts
         and rows % (2 * tile_rows) == 0
-        and parts % 2 == 0
+        and parts % group == 0
         and parts <= 16
         and rows <= 128
     )

time: 71.9 us -> 59.8 us (0.83)
  Pallas kernels: 65.9 us -> 55.4 us
  local copies, waits for them, and re-layouts: 4.52 us -> 3.55 us
    pallas_call x1, Pallas kernels: 65.9 us -> 55.4 us  [whole_kernel(): pl.pallas_call(functools.partial(kernel, parts), out_shape=(jax.ShapeDtyp...]
    unnamed x8 -> x2, local copies, waits for them, and re-layouts: 4.52 us -> 3.55 us
where the time goes in v1:
time: 59.8 us; the launch traced here: 59.6 us
  Pallas kernels  55.4 us (93%)
  local copies, waits for them, and re-layouts  3.55 us (6%)
  between operations  0.64 us (1%)
    pallas_call x1, Pallas kernels, whole_kernel(): pl.pallas_call(functools.partial(kernel, parts), out_shape=(jax.ShapeDtyp...  55.4 us
    unnamed x2, local copies, waits for them, and re-layouts  3.55 us

profile of v1, /device:TPU:25, one launch (start us, length us, event | category | flops | bytes accessed | tf_op | source)
XLA Modules:
  0.0 59.6 jit_solution(12710754786644837317)
XLA Ops:
  0.6 55.4 %shard_map.68 = (bf16[128,2048]{1,0:T(8,128)(2,1)}, bf16[128,1024]{1,0:T(8,128)(2,1)}) custom-call(bf16[128,2048]{1,0:T(8,128)(2,1)} %bitcast.3, bf16[128,2048]{1,0:T(8,128)(2,1)} %bitcast.4, bf16[128,1024]{1,0:T(8,128)(2,1)} %f_hbm.1, bf16[17,512,256]{2,1,0:T(8,128)(2,1)} %constant.4.clone.fwd_hbm, bf16[17,512,256]{2,1,0:T(8,128)(2,1)} %constant.5.clone.inv_hbm), custom_call_target="tpu_custom_call" | custom-call | tf_op jit(solution)/shard_map/pallas_call | solution.py:532
  56.1 1.9 %copy.9 = bf16[1,128,2048]{2,1,0:T(8,128)(2,1)} copy(bf16[1,128,2048]{2,1,0:T(8,128)(2,1)} %bitcast.5) | data formatting | bytes 1048576
  58.0 1.7 %copy.10 = bf16[128,1024]{1,0:T(8,128)(2,1)} copy(bf16[128,1024]{1,0:T(8,128)(2,1)} %get-tuple-element.9) | data formatting | bytes 524288

commit v2 on v1

--- a/solution.py
+++ b/solution.py
@@ -278,7 +278,6 @@
 ):
     me_s, me_d = lax.axis_index("seq"), lax.axis_index("dp")
     everyone = 2 * parts
-    me = me_s * 2 + me_d
     own = me_d * parts + me_s
     rows = x_ref.shape[0]
     half = rows // 2
@@ -298,18 +297,14 @@
 
         lax.fori_loop(start, stop, step, 0)
 
-    def partner(o):
-        other = lax.rem(me + o, everyone)
-        return lax.div(other, 2), lax.rem(other, 2)
-
     barrier = pltpu.get_barrier_semaphore()
-
-    def greet(o):
-        s, d = partner(o)
-        pl.semaphore_signal(
-            barrier, inc=1, device_id=(s, d), device_id_type=pl.DeviceIdType.MESH
-        )
-
+    for ahead in range(parts):
+        s = me_s + ahead
+        s = jnp.where(s >= parts, s - parts, s)
+        for d in (1 - me_d, me_d)[: 2 if ahead else 1]:
+            pl.semaphore_signal(
+                barrier, inc=1, device_id=(s, d), device_id_type=pl.DeviceIdType.MESH
+            )
     f_copy = pltpu.make_async_copy(f_hbm, f_ref, table_sem.at[2])
     g_copy = pltpu.make_async_copy(g_hbm, g_ref, table_sem.at[3])
     x_copy = pltpu.make_async_copy(x_hbm, x_ref, table_sem.at[4])
@@ -318,11 +313,10 @@
     f_copy.start()
     g_copy.start()
     x_copy.start()
-    loop(1, everyone, greet)
     fwd_copy.start()
     inv_copy.start()
 
-    def pack(source, target, m):
+    def pack_pair(source, target, m):
         column = pl.ds(pl.multiple_of(m * lanes, lanes), lanes)
         first, second = swap(
             low_half,
@@ -331,6 +325,9 @@
         )
         target[2 * m] = first.astype(bf16)
         target[2 * m + 1] = second.astype(bf16)
+
+    def pack(source, target):
+        loop(0, source.shape[1] // lanes, functools.partial(pack_pair, source, target))
 
     def unpack(source, target):
         def step(m):
@@ -357,7 +354,8 @@
             ).start()
 
         def pair(step, before):
-            m = lax.rem(lax.div(mine, 2) + step, count // 2)
+            m = lax.div(mine, 2) + step
+            m = jnp.where(m >= count // 2, m - count // 2, m)
             if before is not None:
                 before(m)
             for i in (2 * m, 2 * m + 1):
@@ -378,8 +376,12 @@
         )
         return start_all, everything.wait_recv, everything.wait_send
 
+    def device_at(i):
+        d = jnp.where(i >= parts, 1, 0)
+        return i - d * parts, d
+
     def to_all(*refs):
-        return exchange(*refs, own, lambda i: (lax.rem(i, parts), lax.div(i, parts)))
+        return exchange(*refs, own, device_at)
 
     def to_row(*refs):
         return exchange(*refs, me_s, lambda i: (i, me_d))
@@ -391,12 +393,13 @@
     gf_start, gf_wait, gf_sent = to_row(gfs, gfr, gfs_sem, gfr_sem)
 
     f_copy.wait()
+    pack(f_ref, fs)
     g_copy.wait()
+    x_copy.wait()
     pl.semaphore_wait(barrier, everyone - 1)
-    f_start(lambda m: pack(f_ref, fs, m))
-    g_start(lambda m: pack(g_ref, gs, m))
-    x_copy.wait()
-    x_start(lambda m: pack(x_ref, xs, m))
+    f_start()
+    g_start(functools.partial(pack_pair, g_ref, gs))
+    x_start(functools.partial(pack_pair, x_ref, xs))
 
     zeros = jnp.zeros((rows, lanes), bf16)
 

time: 59.8 us -> 59.4 us (level)
  no operation moved by 1% of the time
where the time goes in v2:
time: 59.4 us; the launch traced here: 59.2 us
  Pallas kernels  55 us (93%)
  local copies, waits for them, and re-layouts  3.55 us (6%)
  between operations  0.64 us (1%)
    pallas_call x1, Pallas kernels, whole_kernel(): pl.pallas_call(functools.partial(kernel, parts), out_shape=(jax.ShapeDtyp...  55 us
    unnamed x2, local copies, waits for them, and re-layouts  3.55 us

profile of v2, /device:TPU:25, one launch (start us, length us, event | category | flops | bytes accessed | tf_op | source)
XLA Modules:
  0.0 59.2 jit_solution(11355313125567897535)
XLA Ops:
  0.6 55.0 %shard_map.68 = (bf16[128,2048]{1,0:T(8,128)(2,1)}, bf16[128,1024]{1,0:T(8,128)(2,1)}) custom-call(bf16[128,2048]{1,0:T(8,128)(2,1)} %bitcast.3, bf16[128,2048]{1,0:T(8,128)(2,1)} %bitcast.4, bf16[128,1024]{1,0:T(8,128)(2,1)} %f_hbm.1, bf16[17,512,256]{2,1,0:T(8,128)(2,1)} %constant.4.clone.fwd_hbm, bf16[17,512,256]{2,1,0:T(8,128)(2,1)} %constant.5.clone.inv_hbm), custom_call_target="tpu_custom_call" | custom-call | tf_op jit(solution)/shard_map/pallas_call | solution.py:535
  55.6 1.9 %copy.9 = bf16[1,128,2048]{2,1,0:T(8,128)(2,1)} copy(bf16[1,128,2048]{2,1,0:T(8,128)(2,1)} %bitcast.5) | data formatting | bytes 1048576
  57.5 1.7 %copy.10 = bf16[128,1024]{1,0:T(8,128)(2,1)} copy(bf16[128,1024]{1,0:T(8,128)(2,1)} %get-tuple-element.9) | data formatting | bytes 524288
